TPU v7x, 32 devices: a whole 2x2x4 slice. The times are simulated.
32 devices in a mesh: dp: 4 (over z), tm: 2 (over core), rows: 4 (over y, x).
Axes of the slice: x: 2, y: 2, z: 4, core: 2. Of those that a mesh axis runs over, the one named last changes fastest.
Arguments:
- latent: bfloat16 [4, 4, 8, 176, 256], P('dp', 'tm', 'rows'), may hold values from -12 to 12, as said below
- gamma: float32 [256], replicated, may hold values from 0.1 to 1.9
- beta: float32 [256], replicated, may hold values from -3 to 3
- weight: bfloat16 [3, 3, 3, 256, 256], replicated, may hold values from -0.078125 to 0.078125
- bias: float32 [256], replicated, may hold values from -3 to 3
- cotangent: bfloat16 [4, 4, 8, 176, 256], P('dp', 'tm', 'rows'), may hold values from -0.039794922 to 0.039794922
Outputs:
- output: bfloat16 [4, 4, 8, 176, 256], P('dp', 'tm', 'rows')
- weight_grad: float32 [2304, 256], P(('tm', 'rows'))
Inputs may be any that keep to these rules, and one draw needn't show every extreme that they name: `latent`: feature values, with each clip's group variance at least 0.5.
All inputs are finite; a program needn't handle non-finite values.
Results may differ from a plain program's by a relative error of at most 0.0029.
Values may be sent and summed in bfloat16 or wider, within the bound.
No kernel may reach another device: no remote copies, remote signals or barrier semaphores. Data moves between devices by JAX's collectives and lax.ppermute only.
A program may use at most 64 MiB of HBM per device.

v0:
```python
import jax
import jax.numpy as jnp
from jax import lax
from jax.sharding import PartitionSpec as P

GROUPS = 32


def with_halo(block, sides, width):
    for axis, dim in sides:
        count = lax.axis_size(axis)
        forward = [(i, i + 1) for i in range(count - 1)]
        backward = [(target, source) for source, target in forward]
        low = lax.ppermute(
            lax.slice_in_dim(block, block.shape[dim] - width, None, axis=dim), axis, forward
        )
        high = lax.ppermute(lax.slice_in_dim(block, 0, width, axis=dim), axis, backward)
        block = jnp.concatenate([low, block, high], axis=dim)
    return block


def shifted(value, axis, steps):
    count = lax.axis_size(axis)
    initial, last = (max(0, -steps), min(count, count - steps))
    return lax.ppermute(value, axis, [(source, source + steps) for source in range(initial, last)])


def build_patches(padded, frames, height, width):
    pieces = []
    for offset_t in range(3):
        for offset_h in range(3):
            for offset_w in range(3):
                pieces.append(
                    padded[
                        :,
                        offset_t : offset_t + frames,
                        offset_h : offset_h + height,
                        offset_w : offset_w + width,
                        :,
                    ]
                )
    return jnp.concatenate(pieces, axis=-1)


def body(latent, gamma, beta, weight, bias, cotangent):
    nclip, frames, height, width, chans = latent.shape
    per_group = chans // GROUPS
    latent_f = latent.astype(jnp.float32)
    grouped = latent_f.reshape(nclip, frames * height * width, GROUPS, per_group)
    part_sum = jnp.sum(grouped, axis=(1, 3))
    part_squares = jnp.sum(grouped * grouped, axis=(1, 3))
    total_sum, total_squares = lax.psum((part_sum, part_squares), ("tm", "rows"))
    count = frames * height * width * per_group * lax.axis_size("tm") * lax.axis_size("rows")
    mean = total_sum / count
    var = total_squares / count - mean * mean
    inverse = lax.rsqrt(var + 1e-06)
    normed = ((grouped - mean[:, None, :, None]) * inverse[:, None, :, None]).reshape(latent.shape)
    act = jax.nn.silu(normed * gamma + beta).astype(jnp.bfloat16)
    rimmed = with_halo(act, (("rows", 2),), 1)
    rimmed = jnp.pad(rimmed, ((0, 0), (0, 0), (0, 0), (1, 1), (0, 0)))
    earlier = shifted(rimmed, "tm", 1)
    leading = jnp.broadcast_to(rimmed[:, :1], earlier.shape)
    earlier = jnp.where(lax.axis_index("tm") == 0, leading, earlier)
    padded = jnp.concatenate([earlier, rimmed], axis=1)
    patches = build_patches(padded, frames, height, width).reshape(
        nclip * frames * height * width, 27 * chans
    )
    kernel = weight.reshape(27 * chans, chans)
    conv = jnp.dot(patches, kernel, preferred_element_type=jnp.float32).reshape(latent.shape)
    output = (latent_f + bias + conv).astype(jnp.bfloat16)
    flat_grad = cotangent.reshape(-1, chans)
    earliest = patches[:, : 9 * chans]
    shard = lax.psum_scatter(
        lax.dot_general(
            earliest, flat_grad, (((0,), (0,)), ((), ())), preferred_element_type=jnp.float32
        ),
        ("tm", "rows"),
        scatter_dimension=0,
        tiled=True,
    )
    weight_grad = lax.psum(shard, "dp")
    return (output, weight_grad)


def solution(mesh):
    placed = (
        P("dp", "tm", "rows", None, None),
        P(),
        P(),
        P(),
        P(),
        P("dp", "tm", "rows", None, None),
    )
    return jax.shard_map(
        body,
        mesh=mesh,
        in_specs=placed,
        out_specs=(P("dp", "tm", "rows", None, None), P(("tm", "rows"), None)),
        check_vma=False,
    )
```

profile of v0, /device:TPU:0, one launch (start us, length us, event | category | flops | bytes accessed | tf_op | source)
XLA Modules:
  0.0 151.3 jit_solution(16156035599880228167)
XLA Ops:
  7.2 1.8 %convert_reduce_fusion = (f32[256]{0:T(256)}, f32[256]{0:T(256)}) fusion(bf16[1,2,2,176,256]{4,3,2,1,0:T(8,128)(2,1)} %param.6), kind=kLoop, calls=%fused_computation.27 | loop fusion | flops 720384 | bytes 362496 | tf_op jit(solution)/shard_map/reduce_sum | solution.py:50
  9.1 0.8 reduce_sum.26
  9.8 1.4 reduce_sum.41
  11.8 0.8 reduce_sum.42
  12.7 15.9 %all-reduce.1 = (f32[1,32]{1,0:T(1,128)S(1)}, f32[1,32]{1,0:T(1,128)S(1)}) all-reduce(f32[1,32]{1,0:T(1,128)S(1)} %bitcast.35, f32[1,32]{1,0:T(1,128)} %bitcast.34), channel_id=1, replica_groups=mesh['dp'=4,'tm'=2,'rows'=4] {'tm','rows'}, use_global_device_ids=true, to_apply=%region_5.6 | all-reduce | flops 64 | bytes 512 | tf_op jit(solution)/shard_map/psum | solution.py:52
  29.2 0.7 sub.23
  29.8 0.7 mul.46
  31.2 1.3 fusion.27
  32.5 3.3 %collective-permute-start = (bf16[1,2,1,176,256]{4,3,2,1,0:T(8,128)(2,1)S(1)}, bf16[1,2,1,176,256]{4,3,2,1,0:T(8,128)(2,1)S(1)}, u32[]{:S(2)}, u32[]{:S(2)}) collective-permute-start(bf16[1,2,1,176,256]{4,3,2,1,0:T(8,128)(2,1)S(1)} %get-tuple-element.6), channel_id=1, source_target_pairs={{0,1},{1,2},{2,3},{4,5},{5,6},{6,7},{8,9},{9,10},{10,11},{12,13},{... | collective-permute-start | bytes 540680 | tf_op jit(solution)/shard_map/ppermute | solution.py:14
  35.8 1.3 collective-permute-start.1
  37.1 1.7 %collective-permute-done = bf16[1,2,1,176,256]{4,3,2,1,0:T(8,128)(2,1)S(1)} collective-permute-done((bf16[1,2,1,176,256]{4,3,2,1,0:T(8,128)(2,1)S(1)}, bf16[1,2,1,176,256]{4,3,2,1,0:T(8,128)(2,1)S(1)}, u32[]{:S(2)}, u32[]{:S(2)}) %collective-permute-start) | collective-permute-done | bytes 180256 | tf_op jit(solution)/shard_map/ppermute | solution.py:14
  38.8 5.9 %collective-permute-done.1 = bf16[1,2,1,176,256]{4,3,2,1,0:T(8,128)(2,1)S(1)} collective-permute-done((bf16[1,2,1,176,256]{4,3,2,1,0:T(8,128)(2,1)S(1)}, bf16[1,2,1,176,256]{4,3,2,1,0:T(8,128)(2,1)S(1)}, u32[]{:S(2)}, u32[]{:S(2)}) %collective-permute-start.1) | collective-permute-done | bytes 180256 | tf_op jit(solution)/shard_map/ppermute | solution.py:17
  44.9 0.9 copy-done.1
  45.8 1.1 copy.8
  46.9 2.2 %collective-permute-start.2 = (bf16[1,2,4,178,256]{4,2,3,1,0:T(4,128)(2,1)}, bf16[1,2,4,178,256]{4,2,3,1,0:T(4,128)(2,1)}, u32[]{:S(2)}, u32[]{:S(2)}) collective-permute-start(bf16[1,2,4,178,256]{4,2,3,1,0:T(4,128)(2,1)} %copy.8), channel_id=1, source_target_pairs={{0,4},{1,5},{2,6},{3,7},{8,12},{9,13},{10,14},{11,15},{16,20},{17,... | collective-permute-start | bytes 2187272 | tf_op jit(solution)/shard_map/ppermute | solution.py:25
  49.1 1.1 slice_bitcast_fusion
  50.4 1.2 copy_select_fusion
  52.4 1.0 fusion.32
  54.8 3.7 %copy-done.10 = bf16[1,2,2,176,6912]{4,3,2,1,0:T(8,128)(2,1)} copy-done((bf16[1,2,2,176,6912]{4,3,2,1,0:T(8,128)(2,1)}, bf16[1,2,2,176,6912]{4,3,2,1,0:T(8,128)(2,1)S(1)}, u32[]{:S(2)}) %copy-start.10) | copy-done | bytes 9732120
  58.6 2.6 %fusion.2 = f32[2304,256]{1,0:T(8,128)} fusion(bf16[704,256]{1,0:T(8,128)(2,1)S(1)} %bitcast.36, bf16[704,6912]{1,0:T(8,128)(2,1)S(1)} %bitcast.33), kind=kOutput, calls=%fused_computation.2 | convolution fusion | flops 830472192 | bytes 5963776 | tf_op jit(solution)/shard_map/dot_general | solution.py:74
  61.2 43.2 %reduce-scatter.2.cloned.1.call-done = f32[288,256]{1,0:T(8,128)} async-done(((f32[2304,256]{1,0:T(8,128)}), f32[288,256]{1,0:T(8,128)}) %reduce-scatter.2.cloned.1.call-update) | async-done | bytes 294928 | tf_op jit(solution)/shard_map/reduce_scatter | solution.py:73
  104.5 7.2 %fusion.11 = bf16[1,2,2,176,256]{4,3,2,1,0:T(8,128)(2,1)} fusion(bf16[6912,256,1,1]{1,0,3,2:T(8,128)(2,1)S(1)} %bitcast.32, bf16[1,2,2,176,6912]{4,3,2,1,0:T(8,128)(2,1)} %copy-done.10, bf16[1,2,2,176,256]{4,3,2,1,0:T(8,128)(2,1)} %param.6, f32[256]{0:T(256)S(1)} %copy-done.16), kind=kOutput, calls=%fused_computation.29 | convolution fusion | flops 2492137472 | bytes 13992960 | tf_op jit(solution)/shard_map/dot_general | solution.py:69
  111.7 31.1 %all-reduce.4.cloned.1.call-done = f32[288,256]{1,0:T(8,128)} async-done(((f32[288,256]{1,0:T(8,128)}), f32[288,256]{1,0:T(8,128)}) %all-reduce.4.cloned.1.call-update) | async-done | bytes 294928 | tf_op jit(solution)/shard_map/psum | solution.py:81
  142.8 1.7 %copy.39 = f32[288,256]{1,0:T(8,128)} copy(f32[288,256]{1,0:T(8,128)} %all-reduce.4.cloned.1.call-done) | data formatting | bytes 589824
  (69 shorter events, 4.3 us)
Async XLA Ops:
  7.2 97.3 %copy-start = (bf16[3,3,3,256,256]{4,3,2,1,0:T(8,128)(2,1)S(1)}, bf16[3,3,3,256,256]{4,3,2,1,0:T(8,128)(2,1)}, u32[]{:S(2)}) copy-start(bf16[3,3,3,256,256]{4,3,2,1,0:T(8,128)(2,1)} %param.9) | copy-start | bytes 10616836
  7.2 97.3 %reduce-scatter.2.cloned.1.call-start = ((), (), s32[]{:S(2)}) async-start(), calls=%async_computation.1 | async-start | bytes 2654208 | tf_op jit(solution)/shard_map/reduce_scatter | solution.py:73
  32.5 14.4 %copy-start.3 = (bf16[1,2,2,176,256]{4,3,2,1,0:T(8,128)(2,1)}, bf16[1,2,2,176,256]{4,3,2,1,0:T(8,128)(2,1)S(1)}, u32[]{:S(2)}) copy-start(bf16[1,2,2,176,256]{4,3,2,1,0:T(8,128)(2,1)S(1)} %fusion.27) | copy-start | bytes 1081348
  32.5 6.3 %collective-permute-start = (bf16[1,2,1,176,256]{4,3,2,1,0:T(8,128)(2,1)S(1)}, bf16[1,2,1,176,256]{4,3,2,1,0:T(8,128)(2,1)S(1)}, u32[]{:S(2)}, u32[]{:S(2)}) collective-permute-start(bf16[1,2,1,176,256]{4,3,2,1,0:T(8,128)(2,1)S(1)} %get-tuple-element.6), channel_id=1, source_target_pairs={{0,1},{1,2},{2,3},{4,5},{5,6},{6,7},{8,9},{9,10},{10,11},{12,13},{... | collective-permute-start | bytes 540680 | tf_op jit(solution)/shard_map/ppermute | solution.py:14
  35.8 8.9 %collective-permute-start.1 = (bf16[1,2,1,176,256]{4,3,2,1,0:T(8,128)(2,1)S(1)}, bf16[1,2,1,176,256]{4,3,2,1,0:T(8,128)(2,1)S(1)}, u32[]{:S(2)}, u32[]{:S(2)}) collective-permute-start(bf16[1,2,1,176,256]{4,3,2,1,0:T(8,128)(2,1)S(1)} %get-tuple-element.7), channel_id=1, source_target_pairs={{1,0},{2,1},{3,2},{5,4},{6,5},{7,6},{9,8},{10,9},{11,10},{13,12},{... | collective-permute-start | bytes 540680 | tf_op jit(solution)/shard_map/ppermute | solution.py:17
  38.8 10.3 %copy-start.8 = (bf16[1,2,1,176,256]{4,3,2,1,0:T(8,128)(2,1)}, bf16[1,2,1,176,256]{4,3,2,1,0:T(8,128)(2,1)S(1)}, u32[]{:S(2)}) copy-start(bf16[1,2,1,176,256]{4,3,2,1,0:T(8,128)(2,1)S(1)} %collective-permute-done) | copy-start | bytes 540676
  44.7 4.4 %copy-start.6 = (bf16[1,2,1,176,256]{4,3,2,1,0:T(8,128)(2,1)}, bf16[1,2,1,176,256]{4,3,2,1,0:T(8,128)(2,1)S(1)}, u32[]{:S(2)}) copy-start(bf16[1,2,1,176,256]{4,3,2,1,0:T(8,128)(2,1)S(1)} %collective-permute-done.1) | copy-start | bytes 540676
  44.9 0.9 copy-start.1
  46.9 3.4 %collective-permute-start.2 = (bf16[1,2,4,178,256]{4,2,3,1,0:T(4,128)(2,1)}, bf16[1,2,4,178,256]{4,2,3,1,0:T(4,128)(2,1)}, u32[]{:S(2)}, u32[]{:S(2)}) collective-permute-start(bf16[1,2,4,178,256]{4,2,3,1,0:T(4,128)(2,1)} %copy.8), channel_id=1, source_target_pairs={{0,4},{1,5},{2,6},{3,7},{8,12},{9,13},{10,14},{11,15},{16,20},{17,... | collective-permute-start | bytes 2187272 | tf_op jit(solution)/shard_map/ppermute | solution.py:25
  49.1 4.2 %copy-start.2 = (bf16[1,2,4,178,256]{4,3,2,1,0:T(8,128)(2,1)S(1)}, bf16[1,2,4,178,256]{4,3,2,1,0:T(8,128)(2,1)}, u32[]{:S(2)}) copy-start(bf16[1,2,4,178,256]{4,3,2,1,0:T(8,128)(2,1)} %copy-done.1) | copy-start | bytes 2187268
  52.0 2.0 %copy-start.4 = (bf16[1,2,2,176,256]{4,3,2,1,0:T(8,128)(2,1)S(1)}, bf16[1,2,2,176,256]{4,3,2,1,0:T(8,128)(2,1)}, u32[]{:S(2)}) copy-start(bf16[1,2,2,176,256]{4,3,2,1,0:T(8,128)(2,1)} %copy-done.3) | copy-start | bytes 1081348
  52.1 2.0 %copy-start.9 = (bf16[1,2,1,176,256]{4,3,2,1,0:T(8,128)(2,1)S(1)}, bf16[1,2,1,176,256]{4,3,2,1,0:T(8,128)(2,1)}, u32[]{:S(2)}) copy-start(bf16[1,2,1,176,256]{4,3,2,1,0:T(8,128)(2,1)} %copy-done.8) | copy-start | bytes 540676
  52.3 2.0 %copy-start.5 = (bf16[1,2,2,176,256]{4,3,2,1,0:T(8,128)(2,1)S(1)}, bf16[1,2,2,176,256]{4,3,2,1,0:T(8,128)(2,1)}, u32[]{:S(2)}) copy-start(bf16[1,2,2,176,256]{4,3,2,1,0:T(8,128)(2,1)} %param.6) | copy-start | bytes 1081348
  52.3 2.0 %copy-start.11 = (f32[256]{0:T(256)S(1)}, f32[256]{0:T(256)}, u32[]{:S(2)}) copy-start(f32[256]{0:T(256)} %sub.23) | copy-start | bytes 3076
  52.3 2.0 %copy-start.12 = (f32[256]{0:T(256)S(1)}, f32[256]{0:T(256)}, u32[]{:S(2)}) copy-start(f32[256]{0:T(256)} %mul.47) | copy-start | bytes 3076
  52.3 2.0 %copy-start.13 = (f32[256]{0:T(256)S(1)}, f32[256]{0:T(256)}, u32[]{:S(2)}) copy-start(f32[256]{0:T(256)} %param.8) | copy-start | bytes 3076
  52.3 2.0 %copy-start.14 = (f32[256]{0:T(256)S(1)}, f32[256]{0:T(256)}, u32[]{:S(2)}) copy-start(f32[256]{0:T(256)} %param.7) | copy-start | bytes 3076
  53.4 1.3 copy-start.7
  53.5 5.1 %copy-start.15 = (bf16[1,2,2,176,256]{4,3,2,1,0:T(8,128)(2,1)S(1)}, bf16[1,2,2,176,256]{4,3,2,1,0:T(8,128)(2,1)}, u32[]{:S(2)}) copy-start(bf16[1,2,2,176,256]{4,3,2,1,0:T(8,128)(2,1)} %param.11) | copy-start | bytes 1081348
  54.1 50.4 %copy-start.16 = (f32[256]{0:T(256)S(1)}, f32[256]{0:T(256)}, u32[]{:S(2)}) copy-start(f32[256]{0:T(256)} %param.10) | copy-start | bytes 3076
  54.8 3.8 %copy-start.10 = (bf16[1,2,2,176,6912]{4,3,2,1,0:T(8,128)(2,1)}, bf16[1,2,2,176,6912]{4,3,2,1,0:T(8,128)(2,1)S(1)}, u32[]{:S(2)}) copy-start(bf16[1,2,2,176,6912]{4,3,2,1,0:T(8,128)(2,1)S(1)} %slice_dynamic-update-slice_fusion) | copy-start | bytes 29196292
  61.2 81.6 %all-reduce.4.cloned.1.call-start = ((), (), s32[]{:S(2)}) async-start(), calls=%async_computation.2 | async-start | bytes 589824 | tf_op jit(solution)/shard_map/psum | solution.py:81
Sparse Core Ops, SparseCore 0:
  61.3 43.0 reduce-scatter.1
  106.9 35.8 all-reduce.3
where the time goes:
time: 152 us; the launch traced here: 151 us
  waiting for transfers between devices  82.1 us (54%)
  blocking collectives  15.9 us (10%)
  between operations  14.5 us (10%)
  local copies, waits for them, and re-layouts  13.9 us (9%)
  matrix products  9.78 us (6%)
  other arithmetic  8.36 us (6%)
  starting transfers between devices  6.82 us (4%)
    reduce_scatter x1, waiting for transfers between devices, body(): lax.psum_scatter(lax.dot_general(earliest, flat_grad, (((0,), (0,)), ((),...  43.2 us
    psum x1, waiting for transfers between devices, body(): weight_grad = lax.psum(shard, 'dp')  31.1 us
    psum x1, blocking collectives, body(): lax.psum((part_sum, part_squares), ('tm', 'rows'))  15.9 us
    unnamed x49, local copies, waits for them, and re-layouts  7.24 us
    dot_general x1, matrix products, body(): jnp.dot(patches, kernel, preferred_element_type=jnp.float32)  7.21 us
    ppermute x1, waiting for transfers between devices, with_halo(): lax.ppermute(lax.slice_in_dim(block, 0, width, axis=dim), axis, backward)  5.92 us
    ppermute x1, starting transfers between devices, with_halo(): lax.ppermute(lax.slice_in_dim(block, block.shape[dim] - width, None, axis...  3.27 us
  transfers between devices with their start and end apart: 5, of which 5 were waited for; matrix products, arithmetic and copies ran while one was open for 5% of the time, Pallas kernels for 0%

commit v1 on v0

--- a/solution.py
+++ b/solution.py
@@ -78,7 +78,7 @@
         scatter_dimension=0,
         tiled=True,
     )
-    weight_grad = lax.psum(shard, "dp")
+    weight_grad = jnp.sum(lax.all_gather(shard, "dp"), axis=0)
     return (output, weight_grad)
 
 

time: 152 us -> 146 us (0.961)
  waiting for transfers between devices: 82.1 us -> 75.9 us
  other arithmetic: 8.36 us -> 10.5 us
  local copies, waits for them, and re-layouts: 13.9 us -> 12.2 us
    psum x1 -> x0, waiting for transfers between devices: 31.1 us -> none  [body(): weight_grad = lax.psum(shard, 'dp')]
    all_gather x0 -> x1, waiting for transfers between devices: none -> 24.8 us  [body(): weight_grad = jnp.sum(lax.all_gather(shard, 'dp'), axis=0)]
    reduce_sum x0 -> x1, other arithmetic: none -> 2.09 us  [body(): weight_grad = jnp.sum(lax.all_gather(shard, 'dp'), axis=0)]
    unnamed x49 -> x48, local copies, waits for them, and re-layouts: 7.24 us -> 5.55 us
  transfers between devices with their start and end apart: 5 -> 5, of which waited for: 5 -> 5; matrix products, arithmetic and copies ran while one was open for 5% -> 6% of each run, Pallas kernels for 0% -> 0%
where the time goes in v1:
time: 146 us; the launch traced here: 145 us
  waiting for transfers between devices  75.9 us (52%)
  blocking collectives  15.9 us (11%)
  between operations  14.5 us (10%)
  local copies, waits for them, and re-layouts  12.2 us (8%)
  other arithmetic  10.5 us (7%)
  matrix products  9.78 us (7%)
  starting transfers between devices  6.82 us (5%)
    reduce_scatter x1, waiting for transfers between devices, body(): lax.psum_scatter(lax.dot_general(earliest, flat_grad, (((0,), (0,)), ((),...  43.2 us
    all_gather x1, waiting for transfers between devices, body(): weight_grad = jnp.sum(lax.all_gather(shard, 'dp'), axis=0)  24.8 us
    psum x1, blocking collectives, body(): lax.psum((part_sum, part_squares), ('tm', 'rows'))  15.9 us
    dot_general x1, matrix products, body(): jnp.dot(patches, kernel, preferred_element_type=jnp.float32)  7.21 us
    ppermute x1, waiting for transfers between devices, with_halo(): lax.ppermute(lax.slice_in_dim(block, 0, width, axis=dim), axis, backward)  5.92 us
    unnamed x48, local copies, waits for them, and re-layouts  5.55 us
    ppermute x1, starting transfers between devices, with_halo(): lax.ppermute(lax.slice_in_dim(block, block.shape[dim] - width, None, axis...  3.27 us
  transfers between devices with their start and end apart: 5, of which 5 were waited for; matrix products, arithmetic and copies ran while one was open for 6% of the time, Pallas kernels for 0%

profile of v1, /device:TPU:0, one launch (start us, length us, event | category | flops | bytes accessed | tf_op | source)
XLA Modules:
  0.0 145.5 jit_solution(7642470866487355200)
XLA Ops:
  7.2 1.8 %convert_reduce_fusion = (f32[256]{0:T(256)}, f32[256]{0:T(256)}) fusion(bf16[1,2,2,176,256]{4,3,2,1,0:T(8,128)(2,1)} %param.6), kind=kLoop, calls=%fused_computation.27 | loop fusion | flops 720384 | bytes 362496 | tf_op jit(solution)/shard_map/reduce_sum | solution.py:50
  9.1 0.8 reduce_sum.34
  9.8 1.4 reduce_sum.50
  11.8 0.8 reduce_sum.51
  12.7 15.9 %all-reduce.1 = (f32[1,32]{1,0:T(1,128)S(1)}, f32[1,32]{1,0:T(1,128)S(1)}) all-reduce(f32[1,32]{1,0:T(1,128)S(1)} %bitcast.37, f32[1,32]{1,0:T(1,128)} %bitcast.36), channel_id=1, replica_groups=mesh['dp'=4,'tm'=2,'rows'=4] {'tm','rows'}, use_global_device_ids=true, to_apply=%region_5.6 | all-reduce | flops 64 | bytes 512 | tf_op jit(solution)/shard_map/psum | solution.py:52
  29.2 0.7 sub.23
  29.8 0.7 mul.46
  31.2 1.3 fusion.27
  32.5 3.3 %collective-permute-start = (bf16[1,2,1,176,256]{4,3,2,1,0:T(8,128)(2,1)S(1)}, bf16[1,2,1,176,256]{4,3,2,1,0:T(8,128)(2,1)S(1)}, u32[]{:S(2)}, u32[]{:S(2)}) collective-permute-start(bf16[1,2,1,176,256]{4,3,2,1,0:T(8,128)(2,1)S(1)} %get-tuple-element.6), channel_id=1, source_target_pairs={{0,1},{1,2},{2,3},{4,5},{5,6},{6,7},{8,9},{9,10},{10,11},{12,13},{... | collective-permute-start | bytes 540680 | tf_op jit(solution)/shard_map/ppermute | solution.py:14
  35.8 1.3 collective-permute-start.1
  37.1 1.7 %collective-permute-done = bf16[1,2,1,176,256]{4,3,2,1,0:T(8,128)(2,1)S(1)} collective-permute-done((bf16[1,2,1,176,256]{4,3,2,1,0:T(8,128)(2,1)S(1)}, bf16[1,2,1,176,256]{4,3,2,1,0:T(8,128)(2,1)S(1)}, u32[]{:S(2)}, u32[]{:S(2)}) %collective-permute-start) | collective-permute-done | bytes 180256 | tf_op jit(solution)/shard_map/ppermute | solution.py:14
  38.8 5.9 %collective-permute-done.1 = bf16[1,2,1,176,256]{4,3,2,1,0:T(8,128)(2,1)S(1)} collective-permute-done((bf16[1,2,1,176,256]{4,3,2,1,0:T(8,128)(2,1)S(1)}, bf16[1,2,1,176,256]{4,3,2,1,0:T(8,128)(2,1)S(1)}, u32[]{:S(2)}, u32[]{:S(2)}) %collective-permute-start.1) | collective-permute-done | bytes 180256 | tf_op jit(solution)/shard_map/ppermute | solution.py:17
  44.9 0.9 copy-done.1
  45.8 1.1 copy.8
  46.9 2.2 %collective-permute-start.2 = (bf16[1,2,4,178,256]{4,2,3,1,0:T(4,128)(2,1)}, bf16[1,2,4,178,256]{4,2,3,1,0:T(4,128)(2,1)}, u32[]{:S(2)}, u32[]{:S(2)}) collective-permute-start(bf16[1,2,4,178,256]{4,2,3,1,0:T(4,128)(2,1)} %copy.8), channel_id=1, source_target_pairs={{0,4},{1,5},{2,6},{3,7},{8,12},{9,13},{10,14},{11,15},{16,20},{17,... | collective-permute-start | bytes 2187272 | tf_op jit(solution)/shard_map/ppermute | solution.py:25
  49.1 1.1 slice_bitcast_fusion
  50.4 1.2 copy_select_fusion
  52.4 1.0 fusion.32
  54.8 3.7 %copy-done.10 = bf16[1,2,2,176,6912]{4,3,2,1,0:T(8,128)(2,1)} copy-done((bf16[1,2,2,176,6912]{4,3,2,1,0:T(8,128)(2,1)}, bf16[1,2,2,176,6912]{4,3,2,1,0:T(8,128)(2,1)S(1)}, u32[]{:S(2)}) %copy-start.10) | copy-done | bytes 9732120
  58.6 2.6 %fusion.2 = f32[2304,256]{1,0:T(8,128)} fusion(bf16[704,256]{1,0:T(8,128)(2,1)S(1)} %bitcast.38, bf16[704,6912]{1,0:T(8,128)(2,1)S(1)} %bitcast.35), kind=kOutput, calls=%fused_computation.2 | convolution fusion | flops 830472192 | bytes 5963776 | tf_op jit(solution)/shard_map/dot_general | solution.py:74
  61.2 43.2 %reduce-scatter.2.cloned.1.call-done = f32[288,256]{1,0:T(8,128)} async-done(((f32[2304,256]{1,0:T(8,128)}), f32[288,256]{1,0:T(8,128)}) %reduce-scatter.2.cloned.1.call-update) | async-done | bytes 294928 | tf_op jit(solution)/shard_map/reduce_scatter | solution.py:73
  104.5 7.2 %fusion.11 = bf16[1,2,2,176,256]{4,3,2,1,0:T(8,128)(2,1)} fusion(bf16[6912,256,1,1]{1,0,3,2:T(8,128)(2,1)S(1)} %bitcast.33, bf16[1,2,2,176,6912]{4,3,2,1,0:T(8,128)(2,1)} %copy-done.10, bf16[1,2,2,176,256]{4,3,2,1,0:T(8,128)(2,1)} %param.6, f32[256]{0:T(256)S(1)} %copy-done.16), kind=kOutput, calls=%fused_computation.29 | convolution fusion | flops 2492137472 | bytes 13992960 | tf_op jit(solution)/shard_map/dot_general | solution.py:69
  111.7 24.8 %all-gather.3.cloned.1.call-done = f32[1152,256]{1,0:T(8,128)} async-done(((f32[288,256]{1,0:T(8,128)}), f32[1152,256]{1,0:T(8,128)}) %all-gather.3.cloned.1.call-update) | async-done | bytes 1179664 | tf_op jit(solution)/shard_map/all_gather | solution.py:81
  136.6 2.1 %reduce_sum.53 = f32[288,256]{1,0:T(8,128)} reduce(f32[4,288,256]{2,1,0:T(8,128)} %bitcast.34, f32[]{:T(128)} %constant.16.clone.1), dimensions={0}, to_apply=%region_7.8 | reduce | flops 221184 | bytes 1474564 | tf_op jit(solution)/shard_map/reduce_sum | solution.py:81
  (69 shorter events, 4.3 us)
Async XLA Ops:
  7.2 97.3 %copy-start = (bf16[3,3,3,256,256]{4,3,2,1,0:T(8,128)(2,1)S(1)}, bf16[3,3,3,256,256]{4,3,2,1,0:T(8,128)(2,1)}, u32[]{:S(2)}) copy-start(bf16[3,3,3,256,256]{4,3,2,1,0:T(8,128)(2,1)} %param.9) | copy-start | bytes 10616836
  7.2 97.3 %reduce-scatter.2.cloned.1.call-start = ((), (), s32[]{:S(2)}) async-start(), calls=%async_computation.1 | async-start | bytes 2654208 | tf_op jit(solution)/shard_map/reduce_scatter | solution.py:73
  32.5 14.4 %copy-start.3 = (bf16[1,2,2,176,256]{4,3,2,1,0:T(8,128)(2,1)}, bf16[1,2,2,176,256]{4,3,2,1,0:T(8,128)(2,1)S(1)}, u32[]{:S(2)}) copy-start(bf16[1,2,2,176,256]{4,3,2,1,0:T(8,128)(2,1)S(1)} %fusion.27) | copy-start | bytes 1081348
  32.5 6.3 %collective-permute-start = (bf16[1,2,1,176,256]{4,3,2,1,0:T(8,128)(2,1)S(1)}, bf16[1,2,1,176,256]{4,3,2,1,0:T(8,128)(2,1)S(1)}, u32[]{:S(2)}, u32[]{:S(2)}) collective-permute-start(bf16[1,2,1,176,256]{4,3,2,1,0:T(8,128)(2,1)S(1)} %get-tuple-element.6), channel_id=1, source_target_pairs={{0,1},{1,2},{2,3},{4,5},{5,6},{6,7},{8,9},{9,10},{10,11},{12,13},{... | collective-permute-start | bytes 540680 | tf_op jit(solution)/shard_map/ppermute | solution.py:14
  35.8 8.9 %collective-permute-start.1 = (bf16[1,2,1,176,256]{4,3,2,1,0:T(8,128)(2,1)S(1)}, bf16[1,2,1,176,256]{4,3,2,1,0:T(8,128)(2,1)S(1)}, u32[]{:S(2)}, u32[]{:S(2)}) collective-permute-start(bf16[1,2,1,176,256]{4,3,2,1,0:T(8,128)(2,1)S(1)} %get-tuple-element.7), channel_id=1, source_target_pairs={{1,0},{2,1},{3,2},{5,4},{6,5},{7,6},{9,8},{10,9},{11,10},{13,12},{... | collective-permute-start | bytes 540680 | tf_op jit(solution)/shard_map/ppermute | solution.py:17
  38.8 10.3 %copy-start.8 = (bf16[1,2,1,176,256]{4,3,2,1,0:T(8,128)(2,1)}, bf16[1,2,1,176,256]{4,3,2,1,0:T(8,128)(2,1)S(1)}, u32[]{:S(2)}) copy-start(bf16[1,2,1,176,256]{4,3,2,1,0:T(8,128)(2,1)S(1)} %collective-permute-done) | copy-start | bytes 540676
  44.7 4.4 %copy-start.6 = (bf16[1,2,1,176,256]{4,3,2,1,0:T(8,128)(2,1)}, bf16[1,2,1,176,256]{4,3,2,1,0:T(8,128)(2,1)S(1)}, u32[]{:S(2)}) copy-start(bf16[1,2,1,176,256]{4,3,2,1,0:T(8,128)(2,1)S(1)} %collective-permute-done.1) | copy-start | bytes 540676
  44.9 0.9 copy-start.1
  46.9 3.4 %collective-permute-start.2 = (bf16[1,2,4,178,256]{4,2,3,1,0:T(4,128)(2,1)}, bf16[1,2,4,178,256]{4,2,3,1,0:T(4,128)(2,1)}, u32[]{:S(2)}, u32[]{:S(2)}) collective-permute-start(bf16[1,2,4,178,256]{4,2,3,1,0:T(4,128)(2,1)} %copy.8), channel_id=1, source_target_pairs={{0,4},{1,5},{2,6},{3,7},{8,12},{9,13},{10,14},{11,15},{16,20},{17,... | collective-permute-start | bytes 2187272 | tf_op jit(solution)/shard_map/ppermute | solution.py:25
  49.1 4.2 %copy-start.2 = (bf16[1,2,4,178,256]{4,3,2,1,0:T(8,128)(2,1)S(1)}, bf16[1,2,4,178,256]{4,3,2,1,0:T(8,128)(2,1)}, u32[]{:S(2)}) copy-start(bf16[1,2,4,178,256]{4,3,2,1,0:T(8,128)(2,1)} %copy-done.1) | copy-start | bytes 2187268
  52.0 2.0 %copy-start.4 = (bf16[1,2,2,176,256]{4,3,2,1,0:T(8,128)(2,1)S(1)}, bf16[1,2,2,176,256]{4,3,2,1,0:T(8,128)(2,1)}, u32[]{:S(2)}) copy-start(bf16[1,2,2,176,256]{4,3,2,1,0:T(8,128)(2,1)} %copy-done.3) | copy-start | bytes 1081348
  52.1 2.0 %copy-start.9 = (bf16[1,2,1,176,256]{4,3,2,1,0:T(8,128)(2,1)S(1)}, bf16[1,2,1,176,256]{4,3,2,1,0:T(8,128)(2,1)}, u32[]{:S(2)}) copy-start(bf16[1,2,1,176,256]{4,3,2,1,0:T(8,128)(2,1)} %copy-done.8) | copy-start | bytes 540676
  52.3 2.0 %copy-start.5 = (bf16[1,2,2,176,256]{4,3,2,1,0:T(8,128)(2,1)S(1)}, bf16[1,2,2,176,256]{4,3,2,1,0:T(8,128)(2,1)}, u32[]{:S(2)}) copy-start(bf16[1,2,2,176,256]{4,3,2,1,0:T(8,128)(2,1)} %param.6) | copy-start | bytes 1081348
  52.3 2.0 %copy-start.11 = (f32[256]{0:T(256)S(1)}, f32[256]{0:T(256)}, u32[]{:S(2)}) copy-start(f32[256]{0:T(256)} %sub.23) | copy-start | bytes 3076
  52.3 2.0 %copy-start.12 = (f32[256]{0:T(256)S(1)}, f32[256]{0:T(256)}, u32[]{:S(2)}) copy-start(f32[256]{0:T(256)} %mul.47) | copy-start | bytes 3076
  52.3 2.0 %copy-start.13 = (f32[256]{0:T(256)S(1)}, f32[256]{0:T(256)}, u32[]{:S(2)}) copy-start(f32[256]{0:T(256)} %param.8) | copy-start | bytes 3076
  52.3 2.0 %copy-start.14 = (f32[256]{0:T(256)S(1)}, f32[256]{0:T(256)}, u32[]{:S(2)}) copy-start(f32[256]{0:T(256)} %param.7) | copy-start | bytes 3076
  53.4 1.3 copy-start.7
  53.5 5.1 %copy-start.15 = (bf16[1,2,2,176,256]{4,3,2,1,0:T(8,128)(2,1)S(1)}, bf16[1,2,2,176,256]{4,3,2,1,0:T(8,128)(2,1)}, u32[]{:S(2)}) copy-start(bf16[1,2,2,176,256]{4,3,2,1,0:T(8,128)(2,1)} %param.11) | copy-start | bytes 1081348
  54.1 50.4 %copy-start.16 = (f32[256]{0:T(256)S(1)}, f32[256]{0:T(256)}, u32[]{:S(2)}) copy-start(f32[256]{0:T(256)} %param.10) | copy-start | bytes 3076
  54.8 3.8 %copy-start.10 = (bf16[1,2,2,176,6912]{4,3,2,1,0:T(8,128)(2,1)}, bf16[1,2,2,176,6912]{4,3,2,1,0:T(8,128)(2,1)S(1)}, u32[]{:S(2)}) copy-start(bf16[1,2,2,176,6912]{4,3,2,1,0:T(8,128)(2,1)S(1)} %slice_dynamic-update-slice_fusion) | copy-start | bytes 29196292
  61.2 75.4 %all-gather.3.cloned.1.call-start = ((), (), s32[]{:S(2)}) async-start(), calls=%async_computation.2 | async-start | bytes 1474560 | tf_op jit(solution)/shard_map/all_gather | solution.py:81
Sparse Core Ops, SparseCore 0:
  61.3 43.0 reduce-scatter.1
  106.1 30.4 all-gather.2
